TPU v7x, 32 devices: a whole 2x2x4 slice. The times are simulated.
32 devices in a mesh: groups: 2 (over y), lon: 4 (over z), lat: 2 (over x), sub: 2 (over core).
Axes of the slice: x: 2, y: 2, z: 4, core: 2. Of those that a mesh axis runs over, the one named last changes fastest.
Arguments:
- tokens: bfloat16 [512, 200, 384], P(('groups', 'lat', 'lon')), parts along dimension 0, may hold values from -130 to 130, as said below
- land_bits: int32 [512, 200], P(('groups', 'lat', 'lon')), parts along dimension 0, may hold values from 0 to 1, as said below
- ocean_list: int32 [4, 128], P(('groups', 'lat')), parts along dimension 0, may hold values from 0 to 128, as said below
- w_qkv: bfloat16 [2, 3, 384, 384], P(None, None, None, 'sub'), as said below
- w_out: bfloat16 [2, 384, 384], P(None, 'sub'), may hold values from -0.3125 to 0.3125
Outputs:
- advanced: bfloat16 [512, 200, 384], P(('groups', 'lat', 'lon')), parts along dimension 0
There are 2 independent parts, one for each index of `groups`. A program takes and returns all parts, laid end to end along the dimension named above; an argument that names none is the same for every part. Nothing has to cross between parts.
Inputs may be any that keep to these rules, and one draw needn't show every extreme that they name: `ocean_list`: each row lists its band's ocean windows in increasing order and then holds 128. A row lists at least 72 and at most 96 windows; some row lists exactly 96. In each window row of a band the listed windows form one run along longitude, which may wrap around. `land_bits`: every token of a window that its band's row of ocean_list does not list is land; in listed windows about a quarter of the tokens are land. `tokens`: finite values. `w_qkv`: entries lie within 165 / sqrt(384) in magnitude.
All inputs are finite; a program needn't handle non-finite values.
Results may differ from a plain program's by a relative error of at most 0.013.
Values may be sent and summed in bfloat16 or wider, within the bound.
A program may use at most 64 MiB of HBM per device.

v0:
```python
import functools

import jax
import jax.numpy as jnp
import numpy as np
from jax import lax
from jax.experimental import pallas as pl
from jax.experimental.pallas import tpu as pltpu
from jax.sharding import PartitionSpec as P

HD = 32
WH = 10
WW = 20
P_SIZE = WH * WW
ROWS = 4
PAD = 208
QR = 64
QT = 50
MESH = pl.DeviceIdType.MESH
SCALE = float(HD ** -0.5 * np.log2(np.e))
NEG = -1e30


def tables():
    token = np.arange(P_SIZE)
    i, j = token // WW, token % WW
    quad = (i // (WH // 2)) * 2 + j // (WW // 2)
    place = (i % (WH // 2)) * (WW // 2) + j % (WW // 2)
    split = np.zeros((4 * QR, PAD + 16), np.float32)
    split[quad * QR + place, token] = 1
    split[np.arange(4) * QR + QT, PAD + np.arange(4)] = 1
    join = np.zeros((PAD, 4 * QR), np.float32)
    join[token, quad * QR + place] = 1
    pick = np.zeros((PAD, 4 * QR), np.float32)
    pick[token, quad * QR + QT] = 1
    gather = np.zeros((16, 4 * QR), np.float32)
    gather[np.arange(4), np.arange(4) * QR + QT] = 1
    lane = np.zeros((PAD, 128), np.float32)
    lane[token, place] = 1
    member = np.zeros((16, PAD), np.float32)
    member[quad, token] = 1
    eye = np.eye(PAD, P_SIZE, dtype=np.float32)
    bf = jnp.bfloat16
    return (
        jnp.asarray(split, bf), jnp.asarray(join, bf), jnp.asarray(pick, bf),
        jnp.asarray(gather, bf), jnp.asarray(lane, bf), jnp.asarray(member, bf), jnp.asarray(eye),
    )


def mm(a, b):
    return jnp.dot(a, b, preferred_element_type=jnp.float32)


def mm_t(a, b):
    return lax.dot_general(a, b, (((1,), (1,)), ((), ())), preferred_element_type=jnp.float32)


def attend(x, land, w_all, wo):
    bf = jnp.bfloat16
    width = wo.shape[0]
    centred = x - jnp.mean(x, axis=-1, keepdims=True)
    var = jnp.mean(centred * centred, axis=-1, keepdims=True)
    normed = (centred * lax.rsqrt(var + 1e-05)).astype(bf)
    qkv = mm(normed, w_all[...])
    q = (qkv[:, :width] * SCALE).astype(bf)
    k = qkv[:, width : 2 * width].astype(bf)
    v = qkv[:, 2 * width :].astype(bf)
    mask = jnp.broadcast_to(land * NEG, (PAD, PAD))
    head = lax.broadcasted_iota(jnp.int32, (1, 128), 1) // HD
    ones = jnp.ones((PAD, 128), bf)
    outs = []
    for low in range(0, width, 128):
        query, key, value = (t[:, low : low + 128] for t in (q, k, v))
        total = None
        for h in range(128 // HD):
            own = jnp.broadcast_to(jnp.where(head == h, 1.0, 0.0).astype(bf), (PAD, 128))
            scores = mm_t(query * own, key) + mask
            top = jnp.max(scores, axis=1, keepdims=True)
            powers = jnp.exp2(scores - top).astype(bf)
            mixed = mm(powers, jnp.concatenate([value * own, ones], axis=1))
            mixed = mixed[:, :128] * (1.0 / mixed[:, 128:])
            total = mixed if total is None else total + mixed
        outs.append(total.astype(bf))
    return mm(jnp.concatenate(outs, axis=1), wo[...])


def kernel(
    tokens, land_rows, listed_row, w_qkv, w_out, split, join, pick, gather, lane, member, eye,
    out,
    toks, wq_far, wo_far, w_buf, wo_buf, e, g, res,
    tok_sem, w_send, w_recv, col_send, col_recv, row_send, row_recv, dia_send, dia_recv,
    bcol_send, bcol_recv, brow_send, brow_recv, bdia_send, bdia_recv,
    o_send, o_recv, o_loc,
):
    bf = jnp.bfloat16
    wins = toks.shape[0]
    cols = wins // ROWS
    feat = toks.shape[2]
    half = w_qkv.shape[3]
    lon, lat, sub = lax.axis_index("lon"), lax.axis_index("lat"), lax.axis_index("sub")
    nlon, nlat, nsub = lax.axis_size("lon"), lax.axis_size("lat"), lax.axis_size("sub")
    spot = lon * nsub + sub
    after = lax.rem(spot + 1, nlon * nsub)
    before = lax.rem(spot + nlon * nsub - 1, nlon * nsub)
    up = lax.rem(lat + nlat - 1, nlat)
    down = lax.rem(lat + 1, nlat)
    mate = {"sub": 1 - sub}
    right = {"lon": after // nsub, "sub": lax.rem(after, nsub)}
    left = {"lon": before // nsub, "sub": lax.rem(before, nsub)}
    above, below = {"lat": up}, {"lat": down}
    left_up = dict(left, lat=up)
    right_down = dict(right, lat=down)
    base = sub * wins

    def load(c):
        return pltpu.make_async_copy(
            tokens.at[pl.ds(base + c * ROWS, ROWS)], toks.at[pl.ds(c * ROWS, ROWS)], tok_sem.at[c]
        )

    for c in range(cols):
        load(c).start()

    barrier = pltpu.get_barrier_semaphore()
    greeted = (mate, right, left, above, below, left_up, right_down)
    for other in greeted:
        pl.semaphore_signal(barrier, inc=1, device_id=other, device_id_type=MESH)
    pl.semaphore_wait(barrier, len(greeted))

    def send(src, dst, s, r, to):
        return pltpu.make_async_remote_copy(
            src_ref=src, dst_ref=dst, send_sem=s, recv_sem=r, device_id=to, device_id_type=MESH
        )

    weights = []
    for b in range(2):
        weights.append(send(w_qkv.at[b], wq_far.at[b], w_send.at[2 * b], w_recv.at[2 * b], mate))
        weights.append(
            send(w_out.at[b], wo_far.at[b], w_send.at[2 * b + 1], w_recv.at[2 * b + 1], mate)
        )
    for copy in weights:
        copy.start()

    def ready(b):
        for part, (wq, wo) in enumerate(((w_qkv, w_out), (wq_far, wo_far))):
            if part == 1:
                weights[2 * b].wait_recv()
                weights[2 * b + 1].wait_recv()
            low = part * half
            wo_buf[low : low + half] = wo[b]
        for kind in range(3):
            w_buf[:, kind * feat : (kind + 1) * feat] = jnp.concatenate(
                [w_qkv[b, kind], wq_far[b, kind]], axis=1
            )

    def col_out(k):
        return send(
            e.at[0, pl.ds(0, ROWS), 2 * k], e.at[cols, pl.ds(0, ROWS), 2 * k],
            col_send.at[k], col_recv.at[k], left,
        )

    def row_out(c):
        return send(
            e.at[c, 0, pl.ds(0, 2)], e.at[c, ROWS, pl.ds(0, 2)],
            row_send.at[c], row_recv.at[c], above,
        )

    dia_out = send(e.at[0, 0, 0], e.at[cols, ROWS, 0], dia_send, dia_recv, left_up)

    pad_rows = jnp.zeros((PAD - P_SIZE, feat), jnp.float32)
    tail_land = (lax.broadcasted_iota(jnp.int32, (PAD, 1), 0) >= P_SIZE).astype(jnp.float32)
    tail_row = (lax.broadcasted_iota(jnp.int32, (1, PAD), 1) >= P_SIZE).astype(jnp.float32)
    ready(0)

    def one(c, r):
        w = c * ROWS + r
        x = jnp.concatenate([toks[w].astype(jnp.float32), pad_rows], axis=0)
        row = land_rows[base + w].astype(jnp.float32)
        land = jnp.sum(eye[...] * row, axis=1, keepdims=True) + tail_land
        wide = jnp.concatenate([row, jnp.zeros((1, PAD - P_SIZE), jnp.float32)], axis=1)
        land_row = wide + tail_row
        mine = spot * wins + w
        listed = jnp.max(
            jnp.where(listed_row[...] == mine, 1.0, 0.0), axis=1, keepdims=True
        )
        update = attend(x, land_row, w_buf, wo_buf)
        first = (x + update * (listed * (1.0 - land))).astype(bf)
        quads_land = mm((member[...].astype(jnp.float32) * wide).astype(bf), lane[...]).astype(bf)
        quads_land = jnp.concatenate([quads_land, jnp.zeros((16, feat - 128), bf)], axis=1)
        quads = mm(split[...], jnp.concatenate([first, quads_land], axis=0)).astype(bf)
        e[c, r] = quads.reshape(4, QR, feat)

    def first_column(c, carry):
        load(c).wait()

        def step(pair, inner):
            for r in range(2):
                one(c, 2 * pair + r)

            @pl.when(pair == 0)
            def _():
                row_out(c).start()

            return inner

        lax.fori_loop(0, ROWS // 2, step, 0)

        @pl.when(c == 0)
        def _():
            col_out(0).start()
            col_out(1).start()
            dia_out.start()

        return carry

    lax.fori_loop(0, cols, first_column, 0)
    ready(1)
    col_out(0).wait_recv()
    col_out(1).wait_recv()
    dia_out.wait_recv()
    for c in range(cols):
        row_out(c).wait_recv()

    def bcol_out(k):
        return send(
            g.at[cols, pl.ds(1, ROWS), 2 * k + 1], g.at[0, pl.ds(1, ROWS), 2 * k + 1],
            bcol_send.at[k], bcol_recv.at[k], right,
        )

    def brow_out(c):
        return send(
            g.at[c + 1, ROWS, pl.ds(2, 2)], g.at[c + 1, 0, pl.ds(2, 2)],
            brow_send.at[c], brow_recv.at[c], below,
        )

    bdia_out = send(g.at[cols, ROWS, 3], g.at[0, 0, 3], bdia_send, bdia_recv, right_down)

    def two(c, r):
        quads = jnp.concatenate(
            [e[c, r, 3], e[c + 1, r, 2], e[c, r + 1, 1], e[c + 1, r + 1, 0]], axis=0
        )
        x = mm(join[...], quads)
        rows = mm(pick[...], quads[:, :128])
        land = jnp.sum(rows * lane[...].astype(jnp.float32), axis=1, keepdims=True) + tail_land
        spread = mm_t(mm(gather[...], quads[:, :128]).astype(bf), lane[...])
        land_row = jnp.sum(spread * member[...].astype(jnp.float32), axis=0, keepdims=True)
        land_row = land_row + tail_row
        edge = jnp.logical_and(lat == nlat - 1, r == ROWS - 1)
        inside = 1.0 - edge.astype(jnp.float32)
        update = attend(x, land_row, w_buf, wo_buf)
        finished = (x + update * ((1.0 - land) * inside)).astype(bf)
        g[c + 1, r + 1] = mm(split[:, :PAD], finished).astype(bf).reshape(4, QR, feat)

    def mate_out(c):
        return send(
            res.at[pl.ds(c * ROWS, ROWS)], out.at[pl.ds(base + c * ROWS, ROWS)],
            o_send.at[c], o_recv.at[c], mate,
        )

    def own_out(c):
        return pltpu.make_async_copy(
            res.at[pl.ds(c * ROWS, ROWS)], out.at[pl.ds(base + c * ROWS, ROWS)], o_loc.at[c]
        )

    def restore(c):
        def step(r, inner):
            quads = jnp.concatenate(
                [g[c, r, 3], g[c + 1, r, 2], g[c, r + 1, 1], g[c + 1, r + 1, 0]], axis=0
            )
            res[c * ROWS + r] = mm(join[...], quads)[:P_SIZE].astype(bf)
            return inner

        lax.fori_loop(0, ROWS, step, 0)
        mate_out(c).start()
        own_out(c).start()

    def second_column(t, carry):
        c = cols - 1 - t

        def step(pair, inner):
            for u in range(2):
                two(c, ROWS - 1 - u - 2 * pair)

            @pl.when(pair == 0)
            def _():
                brow_out(c).start()

            return inner

        lax.fori_loop(0, ROWS // 2, step, 0)

        @pl.when(t == 0)
        def _():
            bcol_out(0).start()
            bcol_out(1).start()
            bdia_out.start()
            brow_out(cols - 1).wait_recv()

        @pl.when(t > 0)
        def _():
            brow_out(c).wait_recv()
            restore(c + 1)

        return carry

    lax.fori_loop(0, cols, second_column, 0)
    bcol_out(0).wait_recv()
    bcol_out(1).wait_recv()
    bdia_out.wait_recv()
    restore(0)

    for copy in weights + [dia_out, bdia_out] + [f(k) for f in (col_out, bcol_out) for k in (0, 1)]:
        copy.wait_send()
    for c in range(cols):
        row_out(c).wait_send()
        brow_out(c).wait_send()
        own_out(c).wait()
        mate_out(c).wait_send()
        far = (1 - sub) * wins + c * ROWS
        send(
            res.at[pl.ds(c * ROWS, ROWS)], out.at[pl.ds(far, ROWS)],
            o_send.at[c], o_recv.at[c], mate,
        ).wait_recv()


def shards(tokens, land_bits, ocean_list, w_qkv, w_out):
    bf = jnp.bfloat16
    count, size, feat = tokens.shape
    wins = count // lax.axis_size("sub")
    cols = wins // ROWS
    vmem = pl.BlockSpec(memory_space=pltpu.VMEM)
    anywhere = pl.BlockSpec(memory_space=pl.ANY)
    dma = pltpu.SemaphoreType.DMA
    return pl.pallas_call(
        kernel,
        out_shape=jax.ShapeDtypeStruct(tokens.shape, bf),
        in_specs=[anywhere] + [vmem] * 11,
        out_specs=anywhere,
        scratch_shapes=[
            pltpu.VMEM((wins, size, feat), bf),
            pltpu.VMEM(w_qkv.shape, bf),
            pltpu.VMEM(w_out.shape, bf),
            pltpu.VMEM((feat, 3 * feat), bf),
            pltpu.VMEM((feat, feat), bf),
            pltpu.VMEM((cols + 1, ROWS + 1, 4, QR, feat), bf),
            pltpu.VMEM((cols + 1, ROWS + 1, 4, QR, feat), bf),
            pltpu.VMEM((wins, size, feat), bf),
            dma((cols,)), dma((4,)), dma((4,)),
            dma((2,)), dma((2,)), dma((cols,)), dma((cols,)), dma(()), dma(()),
            dma((2,)), dma((2,)), dma((cols,)), dma((cols,)), dma(()), dma(()),
            dma((cols,)), dma((cols,)), dma((cols,)),
        ],
        compiler_params=pltpu.CompilerParams(
            collective_id=0, has_side_effects=True, vmem_limit_bytes=48 * 1024 * 1024
        ),
    )(tokens, land_bits.reshape(count, 1, size), ocean_list, w_qkv, w_out, *tables())


def solution(mesh):
    placed = (
        P(("groups", "lat", "lon"), None, None),
        P(("groups", "lat", "lon"), None),
        P(("groups", "lat"), None),
        P(None, None, None, "sub"),
        P(None, "sub", None),
    )
    return jax.shard_map(
        shards,
        mesh=mesh,
        in_specs=placed,
        out_specs=P(("groups", "lat", "lon"), None, None),
        check_vma=False,
    )
```

profile of v0, /device:TPU:0, one launch (start us, length us, event | category | flops | bytes accessed | tf_op | source)
XLA Modules:
  0.0 86.6 jit_solution(14474561176776760029)
XLA Ops:
  0.0 0.8 reshape.3.land_rows
  0.8 1.5 %copy.13.w_qkv = bf16[2,3,384,192]{3,2,1,0:T(8,128)(2,1)S(1)} copy(bf16[2,3,384,192]{2,3,1,0:T(8,128)(2,1)} %param.15) | data formatting | bytes 1769472 | tf_op args[3]
  2.3 0.0 copy-start
  2.3 1.0 %copy-done = bf16[2,192,384]{2,1,0:T(8,128)(2,1)S(1)} copy-done((bf16[2,192,384]{2,1,0:T(8,128)(2,1)S(1)}, bf16[2,192,384]{2,1,0:T(8,128)(2,1)}, u32[]{:S(2)}) %copy-start) | copy-done | bytes 294936
  3.3 0.0 copy-start.1
  3.3 0.9 %copy-done.1 = f32[208,200]{1,0:T(8,128)S(1)} copy-done((f32[208,200]{1,0:T(8,128)S(1)}, f32[208,200]{1,0:T(8,128)}, u32[]{:S(2)}) %copy-start.1) | copy-done | bytes 166424
  4.2 0.0 copy-start.2
  4.2 0.9 %copy-done.2 = bf16[256,224]{1,0:T(8,128)(2,1)S(1)} copy-done((bf16[256,224]{1,0:T(8,128)(2,1)S(1)}, bf16[256,224]{1,0:T(8,128)(2,1)}, u32[]{:S(2)}) %copy-start.2) | copy-done | bytes 114712
  5.1 0.0 copy-start.3
  5.1 0.9 %copy-done.3 = bf16[208,256]{1,0:T(8,128)(2,1)S(1)} copy-done((bf16[208,256]{1,0:T(8,128)(2,1)S(1)}, bf16[208,256]{1,0:T(8,128)(2,1)}, u32[]{:S(2)}) %copy-start.3) | copy-done | bytes 106520
  6.0 0.0 copy-start.4
  6.0 0.9 %copy-done.4 = bf16[208,256]{1,0:T(8,128)(2,1)S(1)} copy-done((bf16[208,256]{1,0:T(8,128)(2,1)S(1)}, bf16[208,256]{1,0:T(8,128)(2,1)}, u32[]{:S(2)}) %copy-start.4) | copy-done | bytes 106520
  6.9 0.0 copy-start.5
  6.9 0.8 copy-done.5
  7.7 0.0 copy-start.6
  7.7 0.7 copy-done.6
  8.4 0.0 copy-start.7
  8.4 0.7 copy-done.7
  9.1 0.0 copy-start.8
  9.1 0.7 copy-done.8
  9.8 71.6 %shard_map.118 = bf16[32,200,384]{2,1,0:T(8,128)(2,1)} custom-call(bf16[32,200,384]{2,1,0:T(8,128)(2,1)} %tokens.1, s32[32,1,200]{2,1,0:T(1,128)S(1)} %reshape.3.land_rows, s32[1,128]{1,0:T(1,128)S(1)} %copy-done.8, bf16[2,3,384,192]{3,2,1,0:T(8,128)(2,1)S(1)} %copy.13.w_qkv, bf16[2,192,384]{2,1,0:T(8,128)(2,1)S(1)} %copy-done, ...), custom_call_target="tpu_custom_call" | custom-call | tf_op jit(solution)/shard_map/pallas_call | solution.py:333
  81.4 5.1 %copy.15 = bf16[32,200,384]{2,1,0:T(8,128)(2,1)} copy(bf16[32,200,384]{2,1,0:T(8,128)(2,1)} %shard_map.118) | data formatting | bytes 9830400
Async XLA Ops:
  2.3 1.0 %copy-start = (bf16[2,192,384]{2,1,0:T(8,128)(2,1)S(1)}, bf16[2,192,384]{2,1,0:T(8,128)(2,1)}, u32[]{:S(2)}) copy-start(bf16[2,192,384]{2,1,0:T(8,128)(2,1)} %w_out.1) | copy-start | bytes 884740
  3.3 0.9 %copy-start.1 = (f32[208,200]{1,0:T(8,128)S(1)}, f32[208,200]{1,0:T(8,128)}, u32[]{:S(2)}) copy-start(f32[208,200]{1,0:T(8,128)} %constant.20.clone.eye) | copy-start | bytes 499204
  4.2 0.9 %copy-start.2 = (bf16[256,224]{1,0:T(8,128)(2,1)S(1)}, bf16[256,224]{1,0:T(8,128)(2,1)}, u32[]{:S(2)}) copy-start(bf16[256,224]{1,0:T(8,128)(2,1)} %constant.14.clone.split) | copy-start | bytes 344068
  5.1 0.9 %copy-start.3 = (bf16[208,256]{1,0:T(8,128)(2,1)S(1)}, bf16[208,256]{1,0:T(8,128)(2,1)}, u32[]{:S(2)}) copy-start(bf16[208,256]{1,0:T(8,128)(2,1)} %constant.16.clone.pick) | copy-start | bytes 319492
  6.0 0.9 %copy-start.4 = (bf16[208,256]{1,0:T(8,128)(2,1)S(1)}, bf16[208,256]{1,0:T(8,128)(2,1)}, u32[]{:S(2)}) copy-start(bf16[208,256]{1,0:T(8,128)(2,1)} %constant.15.clone.join) | copy-start | bytes 319492
  6.9 0.8 copy-start.5
  7.7 0.7 copy-start.6
  8.4 0.7 copy-start.7
  9.1 0.7 copy-start.8
where the time goes:
time: 87.1 us; the launch traced here: 86.6 us
  Pallas kernels  71.6 us (82%)
  local copies, waits for them, and re-layouts  14.9 us (17%)
    pallas_call x1, Pallas kernels, shards(): pl.pallas_call(kernel, out_shape=jax.ShapeDtypeStruct(tokens.shape, bf),...  71.6 us
    unnamed x20, local copies, waits for them, and re-layouts  14.1 us

commit v1 on v0

--- a/solution.py
+++ b/solution.py
@@ -1,5 +1,3 @@
-import functools
-
 import jax
 import jax.numpy as jnp
 import numpy as np
@@ -40,11 +38,11 @@
     member = np.zeros((16, PAD), np.float32)
     member[quad, token] = 1
     eye = np.eye(PAD, P_SIZE, dtype=np.float32)
-    bf = jnp.bfloat16
-    return (
-        jnp.asarray(split, bf), jnp.asarray(join, bf), jnp.asarray(pick, bf),
-        jnp.asarray(gather, bf), jnp.asarray(lane, bf), jnp.asarray(member, bf), jnp.asarray(eye),
-    )
+    parts = [np.pad(t, ((0, 0), (0, 256 - t.shape[1]))) for t in (split, join, pick, gather, lane, member, eye)]
+    return jnp.asarray(np.concatenate(parts), jnp.bfloat16)
+
+
+SPANS = (256, PAD, PAD, 16, PAD, 16, PAD)
 
 
 def mm(a, b):
@@ -85,7 +83,7 @@
 
 
 def kernel(
-    tokens, land_rows, listed_row, w_qkv, w_out, split, join, pick, gather, lane, member, eye,
+    tokens, land_rows, listed_row, w_qkv, w_out, table,
     out,
     toks, wq_far, wo_far, w_buf, wo_buf, e, g, res,
     tok_sem, w_send, w_recv, col_send, col_recv, row_send, row_recv, dia_send, dia_recv,
@@ -93,6 +91,11 @@
     o_send, o_recv, o_loc,
 ):
     bf = jnp.bfloat16
+    views, start = [], 0
+    for tall in SPANS:
+        views.append(table.at[pl.ds(start, tall)])
+        start += tall
+    split, join, pick, gather, lane, member, eye = views
     wins = toks.shape[0]
     cols = wins // ROWS
     feat = toks.shape[2]
@@ -175,7 +178,7 @@
         w = c * ROWS + r
         x = jnp.concatenate([toks[w].astype(jnp.float32), pad_rows], axis=0)
         row = land_rows[base + w].astype(jnp.float32)
-        land = jnp.sum(eye[...] * row, axis=1, keepdims=True) + tail_land
+        land = jnp.sum(eye[:, :P_SIZE].astype(jnp.float32) * row, axis=1, keepdims=True) + tail_land
         wide = jnp.concatenate([row, jnp.zeros((1, PAD - P_SIZE), jnp.float32)], axis=1)
         land_row = wide + tail_row
         mine = spot * wins + w
@@ -184,9 +187,9 @@
         )
         update = attend(x, land_row, w_buf, wo_buf)
         first = (x + update * (listed * (1.0 - land))).astype(bf)
-        quads_land = mm((member[...].astype(jnp.float32) * wide).astype(bf), lane[...]).astype(bf)
+        quads_land = mm((member[:, :PAD].astype(jnp.float32) * wide).astype(bf), lane[:, :128]).astype(bf)
         quads_land = jnp.concatenate([quads_land, jnp.zeros((16, feat - 128), bf)], axis=1)
-        quads = mm(split[...], jnp.concatenate([first, quads_land], axis=0)).astype(bf)
+        quads = mm(split[:, : PAD + 16], jnp.concatenate([first, quads_land], axis=0)).astype(bf)
         e[c, r] = quads.reshape(4, QR, feat)
 
     def first_column(c, carry):
@@ -240,9 +243,9 @@
         )
         x = mm(join[...], quads)
         rows = mm(pick[...], quads[:, :128])
-        land = jnp.sum(rows * lane[...].astype(jnp.float32), axis=1, keepdims=True) + tail_land
-        spread = mm_t(mm(gather[...], quads[:, :128]).astype(bf), lane[...])
-        land_row = jnp.sum(spread * member[...].astype(jnp.float32), axis=0, keepdims=True)
+        land = jnp.sum(rows * lane[:, :128].astype(jnp.float32), axis=1, keepdims=True) + tail_land
+        spread = mm_t(mm(gather[...], quads[:, :128]).astype(bf), lane[:, :128])
+        land_row = jnp.sum(spread * member[:, :PAD].astype(jnp.float32), axis=0, keepdims=True)
         land_row = land_row + tail_row
         edge = jnp.logical_and(lat == nlat - 1, r == ROWS - 1)
         inside = 1.0 - edge.astype(jnp.float32)
@@ -333,7 +336,7 @@
     return pl.pallas_call(
         kernel,
         out_shape=jax.ShapeDtypeStruct(tokens.shape, bf),
-        in_specs=[anywhere] + [vmem] * 11,
+        in_specs=[anywhere] + [vmem] * 5,
         out_specs=anywhere,
         scratch_shapes=[
             pltpu.VMEM((wins, size, feat), bf),
@@ -352,7 +355,7 @@
         compiler_params=pltpu.CompilerParams(
             collective_id=0, has_side_effects=True, vmem_limit_bytes=48 * 1024 * 1024
         ),
-    )(tokens, land_bits.reshape(count, 1, size), ocean_list, w_qkv, w_out, *tables())
+    )(tokens, land_bits.reshape(count, 1, size), ocean_list, w_qkv, w_out, tables())
 
 
 def solution(mesh):

time: 87.1 us -> 82.1 us (0.943)
  local copies, waits for them, and re-layouts: 14.9 us -> 10.1 us
    unnamed x20 -> x8, local copies, waits for them, and re-layouts: 14.1 us -> 9.32 us
where the time goes in v1:
time: 82.1 us; the launch traced here: 81.7 us
  Pallas kernels  71.6 us (87%)
  local copies, waits for them, and re-layouts  10.1 us (12%)
    pallas_call x1, Pallas kernels, shards(): pl.pallas_call(kernel, out_shape=jax.ShapeDtypeStruct(tokens.shape, bf),...  71.6 us
    unnamed x8, local copies, waits for them, and re-layouts  9.32 us

profile of v1, /device:TPU:0, one launch (start us, length us, event | category | flops | bytes accessed | tf_op | source)
XLA Modules:
  0.0 81.7 jit_solution(16592973419734043107)
XLA Ops:
  0.0 0.8 reshape.3.land_rows
  0.8 1.5 %copy.7.w_qkv = bf16[2,3,384,192]{3,2,1,0:T(8,128)(2,1)S(1)} copy(bf16[2,3,384,192]{2,3,1,0:T(8,128)(2,1)} %param.9) | data formatting | bytes 1769472 | tf_op args[3]
  2.3 0.0 copy-start
  2.3 1.1 %copy-done = bf16[1120,256]{1,0:T(8,128)(2,1)S(1)} copy-done((bf16[1120,256]{1,0:T(8,128)(2,1)S(1)}, bf16[1120,256]{1,0:T(8,128)(2,1)}, u32[]{:S(2)}) %copy-start) | copy-done | bytes 573464
  3.4 0.0 copy-start.1
  3.4 1.0 %copy-done.1 = bf16[2,192,384]{2,1,0:T(8,128)(2,1)S(1)} copy-done((bf16[2,192,384]{2,1,0:T(8,128)(2,1)S(1)}, bf16[2,192,384]{2,1,0:T(8,128)(2,1)}, u32[]{:S(2)}) %copy-start.1) | copy-done | bytes 294936
  4.3 0.0 copy-start.2
  4.3 0.7 copy-done.2
  5.0 71.6 %shard_map.64 = bf16[32,200,384]{2,1,0:T(8,128)(2,1)} custom-call(bf16[32,200,384]{2,1,0:T(8,128)(2,1)} %tokens.1, s32[32,1,200]{2,1,0:T(1,128)S(1)} %reshape.3.land_rows, s32[1,128]{1,0:T(1,128)S(1)} %copy-done.2, bf16[2,3,384,192]{3,2,1,0:T(8,128)(2,1)S(1)} %copy.7.w_qkv, bf16[2,192,384]{2,1,0:T(8,128)(2,1)S(1)} %copy-done.1, bf16[1120,256]{1,0:T(8,128)(2,1)S(1)} %copy-done), custom_call_target="tpu_custom_call" | custom-call | tf_op jit(solution)/shard_map/pallas_call | solution.py:336
  76.6 5.1 %copy.9 = bf16[32,200,384]{2,1,0:T(8,128)(2,1)} copy(bf16[32,200,384]{2,1,0:T(8,128)(2,1)} %shard_map.64) | data formatting | bytes 9830400
Async XLA Ops:
  2.3 1.1 %copy-start = (bf16[1120,256]{1,0:T(8,128)(2,1)S(1)}, bf16[1120,256]{1,0:T(8,128)(2,1)}, u32[]{:S(2)}) copy-start(bf16[1120,256]{1,0:T(8,128)(2,1)} %constant.2.clone.table) | copy-start | bytes 1720324
  3.4 1.0 %copy-start.1 = (bf16[2,192,384]{2,1,0:T(8,128)(2,1)S(1)}, bf16[2,192,384]{2,1,0:T(8,128)(2,1)}, u32[]{:S(2)}) copy-start(bf16[2,192,384]{2,1,0:T(8,128)(2,1)} %w_out.1) | copy-start | bytes 884740
  4.3 0.7 copy-start.2
